TPU v7x, 32 devices: a whole 2x2x4 slice. The times are simulated.
32 devices in a mesh: seq: 16 (over z, x, core), kvh: 2 (over y).
Axes of the slice: x: 2, y: 2, z: 4, core: 2. Of those that a mesh axis runs over, the one named last changes fastest.
Arguments:
- queries: bfloat16 [4096, 12288], P('seq', 'kvh'), may hold values from -4 to 4
- keys: bfloat16 [4096, 1024], P('seq', 'kvh'), may hold values from -10 to 10
- values: bfloat16 [4096, 1024], P('seq', 'kvh'), may hold values from -6 to 6
- answer_lengths: int32 [4], replicated, may hold values from 512 to 2048, as said below
Outputs:
- attended: bfloat16 [4096, 12288], P(('seq', 'kvh'))
Inputs may be any that keep to these rules, and one draw needn't show every extreme that they name: `answer_lengths`: every length is a multiple of 256; the lengths sum to 4096; exactly one answer has the largest length 2048, every other one at most (7) * 256.
All inputs are finite; a program needn't handle non-finite values.
Results may differ from a plain program's by a relative error of at most 0.0035.
Values may be sent and summed in bfloat16 or wider, within the bound.
No kernel may reach another device: no remote copies, remote signals or barrier semaphores. Data moves between devices by JAX's collectives and lax.ppermute only.
A program may use at most 64 MiB of HBM per device.

v0:
```python
import math

import jax
import jax.numpy as jnp
from jax import lax
from jax.experimental import pallas as pl
from jax.experimental.pallas import tpu as pltpu
from jax.sharding import PartitionSpec as P

QUERY_PER_KEY = 12
HEAD_WIDTH = 128
GROUP_WIDTH = QUERY_PER_KEY * HEAD_WIDTH
SCALE_LOG2 = math.log2(math.e) / math.sqrt(HEAD_WIDTH)
VMEM_LIMIT = 56 * 1024 * 1024


def attention_kernel(
    meta, q_ref, k_ref, v_ref, out_ref, scores, peak, total, weighted, *, block
):
    rows = q_ref.shape[0]
    low, high, base = meta[0], meta[1], meta[3 + pl.program_id(1)] * rows

    def head_columns(h):
        return slice(h * HEAD_WIDTH, (h + 1) * HEAD_WIDTH)

    def block_rows(slot):
        return pl.ds(pl.multiple_of(slot * block, block), block)

    def score(slot, mask):
        keys = k_ref[block_rows(slot), :]
        for h in range(QUERY_PER_KEY):
            found = lax.dot_general(
                q_ref[:, head_columns(h)],
                keys,
                (((1,), (1,)), ((), ())),
                preferred_element_type=jnp.float32,
            )
            if mask is not None:
                found = jnp.where(mask, found, -1e30)
            scores[slot, h] = found
            widest = found[:, :HEAD_WIDTH]
            for part in range(1, block // HEAD_WIDTH):
                widest = jnp.maximum(widest, found[:, head_columns(part)])
            if mask is not None:
                peak[h] = widest
            else:
                peak[h] = jnp.maximum(peak[h], widest)

    tokens = base + lax.broadcasted_iota(jnp.int32, (rows, block), 0)
    mask = lax.broadcasted_iota(jnp.int32, (rows, block), 1) <= tokens
    score(high, mask)

    @pl.loop(low, high)
    def _(slot):
        score(slot, None)

    for h in range(QUERY_PER_KEY):
        top = jnp.max(peak[h], axis=-1, keepdims=True) * SCALE_LOG2
        peak[h] = jnp.broadcast_to(top, (rows, HEAD_WIDTH))
        total[h] = jnp.zeros((rows, HEAD_WIDTH), jnp.float32)
        weighted[h] = jnp.zeros((rows, HEAD_WIDTH), jnp.float32)

    @pl.loop(low, high + 1)
    def _(slot):
        values = v_ref[block_rows(slot), :]
        for h in range(QUERY_PER_KEY):
            top = peak[h]
            pieces = []
            summed = total[h]
            for part in range(block // HEAD_WIDTH):
                piece = jnp.exp2(scores[slot, h, :, head_columns(part)] * SCALE_LOG2 - top)
                summed = summed + piece
                pieces.append(piece.astype(jnp.bfloat16))
            total[h] = summed
            weighted[h] += jnp.dot(
                jnp.concatenate(pieces, axis=1), values, preferred_element_type=jnp.float32
            )

    for h in range(QUERY_PER_KEY):
        whole = jnp.sum(total[h], axis=-1, keepdims=True)
        out_ref[:, head_columns(h)] = (weighted[h] / whole).astype(out_ref.dtype)


def attend(meta, queries, keys, values, part_rows, part_count, span, block):
    heads = queries.shape[1] // GROUP_WIDTH
    window = span * block
    flops = 4 * part_count * part_rows * queries.shape[1] * window
    grid_spec = pltpu.PrefetchScalarGridSpec(
        num_scalar_prefetch=1,
        grid=(heads, part_count),
        in_specs=[
            pl.BlockSpec((part_rows, GROUP_WIDTH), lambda g, p, meta: (meta[3 + p], g)),
            pl.BlockSpec(
                (pl.Element(window), pl.Element(HEAD_WIDTH)),
                lambda g, p, meta: (
                    pl.multiple_of(meta[2] * block, block),
                    pl.multiple_of(g * HEAD_WIDTH, HEAD_WIDTH),
                ),
            ),
            pl.BlockSpec(
                (pl.Element(window), pl.Element(HEAD_WIDTH)),
                lambda g, p, meta: (
                    pl.multiple_of(meta[2] * block, block),
                    pl.multiple_of(g * HEAD_WIDTH, HEAD_WIDTH),
                ),
            ),
        ],
        out_specs=pl.BlockSpec((part_rows, GROUP_WIDTH), lambda g, p, meta: (p, g)),
        scratch_shapes=[
            pltpu.VMEM((span, QUERY_PER_KEY, part_rows, block), jnp.float32),
            pltpu.VMEM((QUERY_PER_KEY, part_rows, HEAD_WIDTH), jnp.float32),
            pltpu.VMEM((QUERY_PER_KEY, part_rows, HEAD_WIDTH), jnp.float32),
            pltpu.VMEM((QUERY_PER_KEY, part_rows, HEAD_WIDTH), jnp.float32),
        ],
    )
    return pl.pallas_call(
        lambda *refs: attention_kernel(*refs, block=block),
        out_shape=jax.ShapeDtypeStruct((part_count * part_rows, queries.shape[1]), jnp.bfloat16),
        grid_spec=grid_spec,
        compiler_params=pltpu.CompilerParams(vmem_limit_bytes=VMEM_LIMIT),
        cost_estimate=pl.CostEstimate(
            flops=flops,
            bytes_accessed=4 * queries.size + 4 * window * heads * HEAD_WIDTH,
            transcendentals=flops // (4 * HEAD_WIDTH),
        ),
    )(meta, queries, keys, values)


def shards(queries, keys, values, answer_lengths):
    block = queries.shape[0]
    count, groups = lax.axis_size("seq"), lax.axis_size("kvh")
    span = min(12, count // 2)
    mine, group = lax.axis_index("seq"), lax.axis_index("kvh")
    ends = jnp.cumsum(answer_lengths, dtype=jnp.int32)
    start = jnp.max(jnp.where(ends <= mine * block, ends, 0))
    window = jnp.maximum(mine - (span - 1), 0)
    low = start // block - window
    head = [low, mine - window, window]

    all_keys = lax.all_gather(keys, "seq", axis=0, tiled=True)
    all_values = lax.all_gather(values, "seq", axis=0, tiled=True)
    part_rows = block // groups

    def run(parts):
        meta = jnp.stack(head + list(parts)).astype(jnp.int32)
        return attend(
            meta, queries, all_keys, all_values, part_rows, len(parts), span, block
        )

    if groups != 2:
        attended = run([jnp.int32(p) for p in range(groups)])
        return lax.all_to_all(attended, "kvh", split_axis=0, concat_axis=1, tiled=True)
    sent = run([1 - group])
    received = lax.all_gather(sent, "kvh", axis=0)
    kept = run([group])
    others = jnp.where(group == 0, received[1], received[0])
    return jnp.where(
        group == 0,
        jnp.concatenate([kept, others], axis=1),
        jnp.concatenate([others, kept], axis=1),
    )


def solution(mesh):
    in_specs = (P("seq", "kvh"), P("seq", "kvh"), P("seq", "kvh"), P())
    out_specs = P(("seq", "kvh"), None)
    return jax.shard_map(shards, mesh=mesh, in_specs=in_specs, out_specs=out_specs, check_vma=False)
```

profile of v0, /device:TPU:31, one launch (start us, length us, event | category | flops | bytes accessed | tf_op | source)
XLA Modules:
  0.0 196.0 jit_solution(16877281362434104848)
XLA Ops:
  6.5 0.0 all-gather.5.cloned.1.call-start
  6.5 0.7 all-gather.5.cloned.1.call-update
  7.3 0.0 all-gather.7.cloned.1.call-start
  7.3 0.7 all-gather.7.cloned.1.call-update
  8.0 0.0 all-gather.9.cloned.1.call-start
  8.1 0.8 reduce-window.9
  8.9 0.7 fusion
  12.1 0.7 pad_add_fusion
  12.7 0.6 pad_add_fusion.2.refs_0_
  13.3 45.7 %all-gather.5.cloned.1.call-done.refs_2_ = bf16[4096,512]{1,0:T(8,128)(2,1)} async-done(((bf16[256,512]{1,0:T(8,128)(2,1)}), bf16[4096,512]{1,0:T(8,128)(2,1)}) %all-gather.5.cloned.1.call-update) | async-done | bytes 4194320 | tf_op jit(solution)/shard_map/all_gather | solution.py:140
  59.0 51.2 %all-gather.7.cloned.1.call-done.refs_3_ = bf16[4096,512]{1,0:T(8,128)(2,1)} async-done(((bf16[256,512]{1,0:T(8,128)(2,1)}), bf16[4096,512]{1,0:T(8,128)(2,1)}) %all-gather.7.cloned.1.call-update) | async-done | bytes 4194320 | tf_op jit(solution)/shard_map/all_gather | solution.py:141
  110.3 14.7 %shard_map.47 = bf16[128,6144]{1,0:T(8,128)(2,1)} custom-call(s32[4]{0:T(128)} %pad_add_fusion.2.refs_0_, bf16[256,6144]{1,0:T(8,128)(2,1)} %refs_1_.3, bf16[4096,512]{1,0:T(8,128)(2,1)} %all-gather.5.cloned.1.call-done.refs_2_, bf16[4096,512]{1,0:T(8,128)(2,1)} %all-gather.7.cloned.1.call-done.refs_3_), custom_call_target="tpu_custom_call" | custom-call | flops 6442450944 | bytes 10485760 | tf_op jit(solution)/shard_map/pallas_call | solution.py:116
  125.0 0.0 all-gather.9.cloned.1.call-update
  125.0 14.7 %shard_map.46 = bf16[128,6144]{1,0:T(8,128)(2,1)} custom-call(s32[4]{0:T(128)} %get-tuple-element.5.refs_0_, bf16[256,6144]{1,0:T(8,128)(2,1)} %refs_1_.3, bf16[4096,512]{1,0:T(8,128)(2,1)} %all-gather.5.cloned.1.call-done.refs_2_, bf16[4096,512]{1,0:T(8,128)(2,1)} %all-gather.7.cloned.1.call-done.refs_3_), custom_call_target="tpu_custom_call" | custom-call | flops 6442450944 | bytes 10485760 | tf_op jit(solution)/shard_map/pallas_call | solution.py:116
  139.8 0.0 copy-start
  139.8 45.6 %all-gather.9.cloned.1.call-done = bf16[256,6144]{1,0:T(8,128)(2,1)} async-done(((bf16[128,6144]{1,0:T(8,128)(2,1)}), bf16[256,6144]{1,0:T(8,128)(2,1)}) %all-gather.9.cloned.1.call-update) | async-done | bytes 3145744 | tf_op jit(solution)/shard_map/all_gather | solution.py:154
  185.4 2.0 %slice_select_fusion = bf16[128,6144]{1,0:T(8,128)(2,1)S(1)} fusion(bf16[256,6144]{1,0:T(8,128)(2,1)} %all-gather.9.cloned.1.call-done, pred[]{:T(512)S(6)} %eq.4), kind=kLoop, calls=%fused_computation.1 | loop fusion | flops 786432 | bytes 4718593 | tf_op jit(solution)/shard_map/jit(_where)/select_n | solution.py:156
  187.4 0.0 copy-done
  187.4 2.0 %maximum_select_fusion = bf16[128,12288]{1,0:T(8,128)(2,1)} fusion(bf16[128,6144]{1,0:T(8,128)(2,1)S(1)} %slice_select_fusion, bf16[128,6144]{1,0:T(8,128)(2,1)S(1)} %copy-done, pred[]{:T(512)S(6)} %eq.4), kind=kLoop, calls=%fused_computation | loop fusion | flops 14155776 | bytes 6291457 | tf_op jit(solution)/shard_map/jit(_where)/select_n | solution.py:157
Async XLA Ops:
  6.5 52.5 %all-gather.5.cloned.1.call-start = ((), (), s32[]{:S(2)}) async-start(), calls=%async_computation | async-start | bytes 4456448 | tf_op jit(solution)/shard_map/all_gather | solution.py:140
  7.3 103.0 %all-gather.7.cloned.1.call-start = ((), (), s32[]{:S(2)}) async-start(), calls=%async_computation.1 | async-start | bytes 4456448 | tf_op jit(solution)/shard_map/all_gather | solution.py:141
  8.0 177.4 %all-gather.9.cloned.1.call-start = ((), (), s32[]{:S(2)}) async-start(), calls=%async_computation.2 | async-start | bytes 4718592 | tf_op jit(solution)/shard_map/all_gather | solution.py:154
  139.8 47.7 %copy-start = (bf16[128,6144]{1,0:T(8,128)(2,1)S(1)}, bf16[128,6144]{1,0:T(8,128)(2,1)}, u32[]{:S(2)}) copy-start(bf16[128,6144]{1,0:T(8,128)(2,1)} %shard_map.46) | copy-start | bytes 4718596
Sparse Core Ops, SparseCore 0:
  9.5 49.4 all-gather.4
  61.2 49.0 all-gather.6
  125.2 60.1 all-gather.8
where the time goes:
time: 199 us; the launch traced here: 196 us
  waiting for transfers between devices  144 us (72%)
  Pallas kernels  29.5 us (15%)
  between operations  15.6 us (8%)
  other arithmetic  6.87 us (3%)
    all_gather x1, waiting for transfers between devices, shards(): all_values = lax.all_gather(values, 'seq', axis=0, tiled=True)  51.2 us
    all_gather x1, waiting for transfers between devices, shards(): all_keys = lax.all_gather(keys, 'seq', axis=0, tiled=True)  45.7 us
    all_gather x1, waiting for transfers between devices, shards(): received = lax.all_gather(sent, 'kvh', axis=0)  45.6 us
    pallas_call x2, Pallas kernels, attend(): pl.pallas_call(lambda *refs: attention_kernel(*refs, block=block), out_sh...  29.5 us
  transfers between devices with their start and end apart: 3, of which 3 were waited for; matrix products, arithmetic and copies ran while one was open for 1% of the time, Pallas kernels for 8%

commit v1 on v0

v1 whole, which is shorter than its diff:
```python
import math

import jax
import jax.numpy as jnp
from jax import lax
from jax.experimental import pallas as pl
from jax.experimental.pallas import tpu as pltpu
from jax.sharding import PartitionSpec as P

QUERY_PER_KEY = 12
HEAD_WIDTH = 128
GROUP_WIDTH = QUERY_PER_KEY * HEAD_WIDTH
SCALE_LOG2 = math.log2(math.e) / math.sqrt(HEAD_WIDTH)
VMEM_LIMIT = 30 * 1024 * 1024
LOW, HIGH, TOKEN, QUERY_ROW, QUERY_COLUMN, OUT_COLUMN, PIECE_ROW = range(7)


def columns(h):
    return slice(h * HEAD_WIDTH, (h + 1) * HEAD_WIDTH)


def attention_kernel(meta, q_ref, *refs, block, pieces):
    out_ref, window, arrived, scores, peak, total, weighted = refs[-7:]
    rows = q_ref.shape[0]
    low, high, base = meta[LOW], meta[HIGH], meta[TOKEN]
    heads = pl.num_programs(0)
    head = pl.program_id(0)

    @pl.when(head == 0)
    def _():
        copies = []
        at = 0
        for number, piece in enumerate(refs[:pieces]):
            taken = min(piece.shape[0], window.shape[0] - at)
            first = pl.multiple_of(meta[PIECE_ROW] * block, block) if pieces == 1 else 0
            copies.append(
                pltpu.make_async_copy(
                    piece.at[pl.ds(first, taken)], window.at[pl.ds(at, taken)], arrived.at[number]
                )
            )
            at += taken
        for copy in copies:
            copy.start()
        for copy in copies:
            copy.wait()

    def block_of(slot, column):
        rows_of = pl.ds(pl.multiple_of(slot * block, block), block)
        return window[rows_of, pl.ds(pl.multiple_of(column * HEAD_WIDTH, HEAD_WIDTH), HEAD_WIDTH)]

    def score(slot, mask):
        keys = block_of(slot, head)
        for h in range(QUERY_PER_KEY):
            found = lax.dot_general(
                q_ref[:, columns(h)],
                keys,
                (((1,), (1,)), ((), ())),
                preferred_element_type=jnp.float32,
            )
            if mask is not None:
                found = jnp.where(mask, found, -1e30)
            scores[slot, h] = found
            widest = found[:, :HEAD_WIDTH]
            for part in range(1, block // HEAD_WIDTH):
                widest = jnp.maximum(widest, found[:, columns(part)])
            if mask is not None:
                peak[h] = widest
            else:
                peak[h] = jnp.maximum(peak[h], widest)

    tokens = base + lax.broadcasted_iota(jnp.int32, (rows, block), 0)
    mask = lax.broadcasted_iota(jnp.int32, (rows, block), 1) <= tokens
    score(high, mask)

    @pl.loop(low, high)
    def _(slot):
        score(slot, None)

    for h in range(QUERY_PER_KEY):
        top = jnp.max(peak[h], axis=-1, keepdims=True) * SCALE_LOG2
        peak[h] = jnp.broadcast_to(top, (rows, HEAD_WIDTH))
        total[h] = jnp.zeros((rows, HEAD_WIDTH), jnp.float32)
        weighted[h] = jnp.zeros((rows, HEAD_WIDTH), jnp.float32)

    @pl.loop(low, high + 1)
    def _(slot):
        values = block_of(slot, heads + head)
        for h in range(QUERY_PER_KEY):
            top = peak[h]
            found = []
            summed = total[h]
            for part in range(block // HEAD_WIDTH):
                piece = jnp.exp2(scores[slot, h, :, columns(part)] * SCALE_LOG2 - top)
                summed = summed + piece
                found.append(piece.astype(jnp.bfloat16))
            total[h] = summed
            weighted[h] += jnp.dot(
                jnp.concatenate(found, axis=1), values, preferred_element_type=jnp.float32
            )

    for h in range(QUERY_PER_KEY):
        whole = jnp.sum(total[h], axis=-1, keepdims=True)
        out_ref[:, columns(h)] = (weighted[h] / whole).astype(out_ref.dtype)


def attend(meta, queries, pieces, part_rows, span, block, out_width, earlier=()):
    heads = pieces[0].shape[1] // (2 * HEAD_WIDTH)
    slots = min(span + 1, sum(p.shape[0] for p in pieces) // block)
    flops = part_rows * heads * GROUP_WIDTH * span * block // 8
    grid_spec = pltpu.PrefetchScalarGridSpec(
        num_scalar_prefetch=1,
        grid=(heads,),
        in_specs=[
            pl.BlockSpec(
                (part_rows, GROUP_WIDTH),
                lambda g, meta: (meta[QUERY_ROW], meta[QUERY_COLUMN] + g),
            )
        ]
        + [pl.BlockSpec(memory_space=pl.ANY)] * (len(pieces) + len(earlier)),
        out_specs=pl.BlockSpec(
            (part_rows, GROUP_WIDTH), lambda g, meta: (0, meta[OUT_COLUMN] + g)
        ),
        scratch_shapes=[
            pltpu.VMEM((slots * block, 2 * heads * HEAD_WIDTH), jnp.bfloat16),
            pltpu.SemaphoreType.DMA((len(pieces),)),
            pltpu.VMEM((slots, QUERY_PER_KEY, part_rows, block), jnp.float32),
            pltpu.VMEM((QUERY_PER_KEY, part_rows, HEAD_WIDTH), jnp.float32),
            pltpu.VMEM((QUERY_PER_KEY, part_rows, HEAD_WIDTH), jnp.float32),
            pltpu.VMEM((QUERY_PER_KEY, part_rows, HEAD_WIDTH), jnp.float32),
        ],
    )
    return pl.pallas_call(
        lambda *refs: attention_kernel(*refs, block=block, pieces=len(pieces)),
        out_shape=jax.ShapeDtypeStruct((part_rows, out_width), jnp.bfloat16),
        grid_spec=grid_spec,
        compiler_params=pltpu.CompilerParams(vmem_limit_bytes=VMEM_LIMIT),
        cost_estimate=pl.CostEstimate(
            flops=flops,
            bytes_accessed=part_rows * heads * GROUP_WIDTH,
            transcendentals=0,
        ),
    )(meta, queries, *pieces, *earlier)


def place_kernel(meta, kept_ref, *refs):
    count = len(refs) - 2
    received, out_ref, sems = refs[:count], refs[count], refs[count + 1]
    width = received[0].shape[1]
    copies = [
        pltpu.make_async_copy(
            ref, out_ref.at[:, pl.ds(pl.multiple_of(meta[n] * width, width), width)], sems.at[n]
        )
        for n, ref in enumerate(received)
    ]
    for copy in copies:
        copy.start()
    for copy in copies:
        copy.wait()


def place(meta, kept, received):
    return pl.pallas_call(
        place_kernel,
        out_shape=jax.ShapeDtypeStruct(kept.shape, kept.dtype),
        grid_spec=pltpu.PrefetchScalarGridSpec(
            num_scalar_prefetch=1,
            grid=(),
            in_specs=[pl.BlockSpec(memory_space=pl.ANY)] * (1 + len(received)),
            out_specs=pl.BlockSpec(memory_space=pl.ANY),
            scratch_shapes=[pltpu.SemaphoreType.DMA((len(received),))],
        ),
        input_output_aliases={1: 0},
    )(meta, kept, *received)


def as_meta(*entries):
    return jnp.stack([jnp.asarray(e, jnp.int32) for e in entries])


def first_visible(answer_lengths, index, block):
    ends = jnp.cumsum(answer_lengths, dtype=jnp.int32)
    return jnp.max(jnp.where(ends <= index * block, ends, 0)) // block


def shards_whole(queries, keys, values, answer_lengths):
    block = queries.shape[0]
    count, groups = lax.axis_size("seq"), lax.axis_size("kvh")
    span = min(12, count // 2)
    mine = lax.axis_index("seq")
    window = jnp.maximum(mine - (span - 1), 0)
    low = first_visible(answer_lengths, mine, block) - window
    gathered = lax.all_gather(jnp.concatenate([keys, values], 1), "seq", axis=0, tiled=True)
    rows = block // groups
    parts = [
        attend(
            as_meta(low, mine - window, part * rows, part, 0, 0, window),
            queries,
            [gathered],
            rows,
            span - 1,
            block,
            queries.shape[1],
        )
        for part in range(groups)
    ]
    return lax.all_to_all(
        jnp.concatenate(parts, 0), "kvh", split_axis=0, concat_axis=1, tiled=True
    )


def shards(queries, keys, values, answer_lengths):
    block = queries.shape[0]
    count, groups = lax.axis_size("seq"), lax.axis_size("kvh")
    heads = keys.shape[1] // HEAD_WIDTH
    if groups != 2 or heads % 2 or count % 2:
        return shards_whole(queries, keys, values, answer_lengths)
    span = min(12, count // 2)
    mine, group = lax.axis_index("seq"), lax.axis_index("kvh")
    core = mine % 2
    pair = mine - core

    def half(value, which):
        width = value.shape[1] // 2
        return lax.dynamic_slice_in_dim(value, which * width, width, 1)

    def swap(value):
        return lax.ppermute(value, "seq", [(i, i ^ 1) for i in range(count)])

    def shift(value, steps):
        return lax.ppermute(value, "seq", [(i, i + steps) for i in range(count - steps)])

    kept_kv = jnp.concatenate([half(keys, core), half(values, core)], 1)
    other_kv = jnp.concatenate([half(keys, 1 - core), half(values, 1 - core)], 1)
    their_kv = swap(other_kv)
    their_queries = swap(half(queries, 1 - core))
    own = jnp.where(
        core == 0,
        jnp.concatenate([kept_kv, their_kv], 0),
        jnp.concatenate([their_kv, kept_kv], 0),
    )
    items = [own, shift(own, 2), shift(own, 4)]
    for steps in range(3, span // 2):
        items.append(shift(items[steps - 2], 4))
    items.append(shift(items[span // 2 - 2][block:], 4))
    pieces = items[::-1]

    rows = block // groups
    origin = pair - (span - 1)
    own_columns = (heads // 2) * core

    def part(tokens_core, tokens_half, earlier, out_width, out_column):
        index = pair + tokens_core
        theirs = tokens_core is not core
        meta = as_meta(
            first_visible(answer_lengths, index, block) - origin,
            index - origin,
            tokens_half * rows,
            tokens_half,
            0 if theirs else own_columns,
            out_column,
            0,
        )
        return attend(
            meta,
            their_queries if theirs else queries,
            pieces,
            rows,
            span,
            block,
            out_width,
            earlier,
        )

    def send(value, flip_core, flip_group):
        pairs = [
            (i * groups + r, (i ^ flip_core) * groups + (r ^ flip_group))
            for i in range(count)
            for r in range(groups)
        ]
        return lax.ppermute(value, ("seq", "kvh"), pairs)

    width = (heads // 2) * GROUP_WIDTH
    far = part(1 - core, 1 - group, (), width, 0)
    from_far = send(far, 1, 1)
    across = part(core, 1 - group, (far,), width, 0)
    beside = part(1 - core, group, (across,), width, 0)
    from_beside = send(beside, 1, 0)
    from_across = send(across, 0, 1)
    out_columns = (group * 2 + core) * (heads // 2)
    kept = part(core, group, (beside, from_far, from_across), groups * queries.shape[1], out_columns)
    places = as_meta(
        group * 2 + 1 - core, (1 - group) * 2 + core, (1 - group) * 2 + 1 - core
    )
    return place(places, kept, [from_beside, from_across, from_far])


def solution(mesh):
    in_specs = (P("seq", "kvh"), P("seq", "kvh"), P("seq", "kvh"), P())
    out_specs = P(("seq", "kvh"), None)
    return jax.shard_map(shards, mesh=mesh, in_specs=in_specs, out_specs=out_specs, check_vma=False)
```

time: 199 us -> 217 us (1.090)
  Pallas kernels: 29.5 us -> 140 us
  waiting for transfers between devices: 144 us -> 48.7 us
  between operations: 15.6 us -> 5.12 us
  local copies, waits for them, and re-layouts: 0.01 us -> 10.3 us
  starting transfers between devices: 0.08 us -> 9.51 us
  other arithmetic: 6.87 us -> 2.85 us
    all_gather x3 -> x0, waiting for transfers between devices: 143 us -> none  [the longest x1 51.2 us: shards(): all_values = lax.all_gather(values, 'seq', axis=0, tiled=True)]
    pallas_call x2 -> x5, Pallas kernels: 29.5 us -> 140 us  [the longest x1 73.3 us: place(): pl.pallas_call(place_kernel, out_shape=jax.ShapeDtypeStruct(kept.shape, k...]
    ppermute x0 -> x9, waiting for transfers between devices: none -> 48.7 us  [the longest x4 29.7 us: shift(): lax.ppermute(value, 'seq', [(i, i + steps) for i in range(count - steps)])]
    ppermute x0 -> x9, starting transfers between devices: none -> 9.51 us  [the longest x4 5.14 us: shift(): lax.ppermute(value, 'seq', [(i, i + steps) for i in range(count - steps)])]
    unnamed x2 -> x26, local copies, waits for them, and re-layouts: 0.01 us -> 6.5 us
    select_n x2 -> x1, other arithmetic: 4.09 us -> 1.32 us  [shards(): jnp.where(core == 0, jnp.concatenate([kept_kv, their_kv], 0), jnp.concate...]
    dynamic_slice x0 -> x2, local copies, waits for them, and re-layouts: none -> 2.75 us  [half(): return lax.dynamic_slice_in_dim(value, which * width, width, 1)]
  transfers between devices with their start and end apart: 3 -> 9, of which waited for: 3 -> 5; matrix products, arithmetic and copies ran while one was open for 1% -> 2% of each run, Pallas kernels for 8% -> 15%
where the time goes in v1:
time: 217 us; the launch traced here: 216 us
  Pallas kernels  140 us (65%)
  waiting for transfers between devices  48.7 us (22%)
  local copies, waits for them, and re-layouts  10.3 us (5%)
  starting transfers between devices  9.51 us (4%)
  between operations  5.12 us (2%)
  other arithmetic  2.85 us (1%)
    pallas_call x1, Pallas kernels, place(): pl.pallas_call(place_kernel, out_shape=jax.ShapeDtypeStruct(kept.shape, k...  73.3 us
    pallas_call x4, Pallas kernels, attend(): pl.pallas_call(lambda *refs: attention_kernel(*refs, block=block, pieces=...  66.4 us
    ppermute x4, waiting for transfers between devices, shift(): lax.ppermute(value, 'seq', [(i, i + steps) for i in range(count - steps)])  29.7 us
    ppermute x3, waiting for transfers between devices, send(): return lax.ppermute(value, ('seq', 'kvh'), pairs)  15.8 us
    unnamed x26, local copies, waits for them, and re-layouts  6.5 us
    ppermute x4, starting transfers between devices, shift(): lax.ppermute(value, 'seq', [(i, i + steps) for i in range(count - steps)])  5.14 us
  transfers between devices with their start and end apart: 9, of which 5 were waited for; matrix products, arithmetic and copies ran while one was open for 2% of the time, Pallas kernels for 15%

profile of v1, /device:TPU:31, one launch (start us, length us, event | category | flops | bytes accessed | tf_op | source)
XLA Modules:
  0.0 216.2 jit_solution(16011290703841643200)
XLA Ops:
  0.0 2.7 %constant_dynamic-slice_fusion = bf16[256,3072]{1,0:T(8,128)(2,1)} fusion(bf16[256,6144]{1,0:T(8,128)(2,1)} %refs_1_.3, s32[]{:T(128)S(6)} %select_n.53), kind=kLoop, calls=%fused_computation.4 | loop fusion | bytes 3145732 | tf_op jit(solution)/shard_map/dynamic_slice | solution.py:224
  2.7 0.7 collective-permute-start.5
  3.6 3.1 %collective-permute-done = bf16[256,512]{1,0:T(8,128)(2,1)S(1)} collective-permute-done((bf16[256,512]{1,0:T(8,128)(2,1)S(1)}, bf16[256,512]{1,0:T(8,128)(2,1)S(1)}, u32[]{:S(2)}, u32[]{:S(2)}) %collective-permute-start) | collective-permute-done | bytes 262176 | tf_op jit(solution)/shard_map/ppermute | solution.py:227
  6.7 0.7 copy-done.11
  7.4 1.3 maximum_select_fusion.refs_6_
  8.7 1.3 collective-permute-start.3
  10.0 1.3 collective-permute-start.1
  11.3 0.8 copy-done.1
  12.1 12.0 %collective-permute-done.3.refs_5_ = bf16[512,512]{1,0:T(8,128)(2,1)} collective-permute-done((bf16[512,512]{1,0:T(8,128)(2,1)S(1)}, bf16[512,512]{1,0:T(8,128)(2,1)}, u32[]{:S(2)}, u32[]{:S(2)}) %collective-permute-start.3) | collective-permute-done | bytes 524320 | tf_op jit(solution)/shard_map/ppermute | solution.py:230
  24.1 1.3 collective-permute-start.4
  25.4 9.8 %collective-permute-done.1.refs_4_ = bf16[512,512]{1,0:T(8,128)(2,1)S(1)} collective-permute-done((bf16[512,512]{1,0:T(8,128)(2,1)S(1)}, bf16[512,512]{1,0:T(8,128)(2,1)S(1)}, u32[]{:S(2)}, u32[]{:S(2)}) %collective-permute-start.1) | collective-permute-done | bytes 524320 | tf_op jit(solution)/shard_map/ppermute | solution.py:230
  35.2 0.7 slice.4
  35.9 0.8 copy-done.5
  36.7 1.3 collective-permute-start.2
  38.0 0.2 reduce-window.9
  38.2 0.7 fusion.1
  43.8 0.1 stack.80.refs_0_
  44.1 7.9 %collective-permute-done.2.refs_2_ = bf16[256,512]{1,0:T(8,128)(2,1)S(1)} collective-permute-done((bf16[256,512]{1,0:T(8,128)(2,1)}, bf16[256,512]{1,0:T(8,128)(2,1)S(1)}, u32[]{:S(2)}, u32[]{:S(2)}) %collective-permute-start.2) | collective-permute-done | bytes 262176 | tf_op jit(solution)/shard_map/ppermute | solution.py:230
  52.0 1.0 copy-done.2
  53.1 1.0 copy-done.6
  54.1 16.2 %shard_map.46.refs_7_ = bf16[128,3072]{1,0:T(8,128)(2,1)} custom-call(s32[7]{0:T(128)S(1)} %stack.80.refs_0_, bf16[256,3072]{1,0:T(8,128)(2,1)} %collective-permute-done.5.refs_1_, bf16[256,512]{1,0:T(8,128)(2,1)S(1)} %collective-permute-done.2.refs_2_, bf16[512,512]{1,0:T(8,128)(2,1)} %collective-permute-done.4.refs_3_, bf16[512,512]{1,0:T(8,128)(2,1)S(1)} %copy-done.6, ...), custom_call_target="tpu_custom_call" | custom-call | flops 100663296 | bytes 393216 | tf_op jit(solution)/shard_map/pallas_call | solution.py:132
  70.4 17.0 %shard_map.47.refs_7_ = bf16[128,3072]{1,0:T(8,128)(2,1)} custom-call(s32[7]{0:T(128)S(1)} %stack.79.refs_0_, bf16[256,6144]{1,0:T(8,128)(2,1)S(1)} %copy-done, bf16[256,512]{1,0:T(8,128)(2,1)S(1)} %collective-permute-done.2.refs_2_, bf16[512,512]{1,0:T(8,128)(2,1)} %collective-permute-done.4.refs_3_, bf16[512,512]{1,0:T(8,128)(2,1)S(1)} %copy-done.7, ...), custom_call_target="tpu_custom_call" | custom-call | flops 100663296 | bytes 393216 | tf_op jit(solution)/shard_map/pallas_call | solution.py:132
  87.4 0.3 collective-permute-start.7
  87.7 2.4 %collective-permute-start.6 = (bf16[128,3072]{1,0:T(8,128)(2,1)}, bf16[128,3072]{1,0:T(8,128)(2,1)}, u32[]{:S(2)}, u32[]{:S(2)}) collective-permute-start(bf16[128,3072]{1,0:T(8,128)(2,1)} %shard_map.46.refs_7_), channel_id=1, source_target_pairs={{0,3},{1,2},{2,1},{3,0},{4,7},{5,6},{6,5},{7,4},{8,11},{9,10},{10,... | collective-permute-start | bytes 2359304 | tf_op jit(solution)/shard_map/ppermute | solution.py:280
  90.0 16.3 %shard_map.48.refs_7_ = bf16[128,3072]{1,0:T(8,128)(2,1)} custom-call(s32[7]{0:T(128)S(1)} %stack.76.refs_0_, bf16[256,3072]{1,0:T(8,128)(2,1)} %collective-permute-done.5.refs_1_, bf16[256,512]{1,0:T(8,128)(2,1)S(1)} %collective-permute-done.2.refs_2_, bf16[512,512]{1,0:T(8,128)(2,1)} %collective-permute-done.4.refs_3_, bf16[512,512]{1,0:T(8,128)(2,1)S(1)} %copy-done.7, ...), custom_call_target="tpu_custom_call" | custom-call | flops 100663296 | bytes 393216 | tf_op jit(solution)/shard_map/pallas_call | solution.py:132
  106.3 0.9 collective-permute-start.8
  107.4 0.7 pad_add_fusion.meta
  108.1 15.8 %collective-permute-done.6.refs_8_.refs_2_ = bf16[128,3072]{1,0:T(8,128)(2,1)} collective-permute-done((bf16[128,3072]{1,0:T(8,128)(2,1)}, bf16[128,3072]{1,0:T(8,128)(2,1)}, u32[]{:S(2)}, u32[]{:S(2)}) %collective-permute-start.6) | collective-permute-done | bytes 786464 | tf_op jit(solution)/shard_map/ppermute | solution.py:280
  123.9 1.0 copy-done.4
  124.9 1.0 copy-done.8
  126.0 16.9 %shard_map.49.kept_ref = bf16[128,12288]{1,0:T(8,128)(2,1)} custom-call(s32[7]{0:T(128)S(1)} %stack.73.refs_0_, bf16[256,6144]{1,0:T(8,128)(2,1)S(1)} %copy-done, bf16[256,512]{1,0:T(8,128)(2,1)S(1)} %collective-permute-done.2.refs_2_, bf16[512,512]{1,0:T(8,128)(2,1)} %collective-permute-done.4.refs_3_, bf16[512,512]{1,0:T(8,128)(2,1)S(1)} %copy-done.8, ...), custom_call_target="tpu_custom_call" | custom-call | flops 100663296 | bytes 393216 | tf_op jit(solution)/shard_map/pallas_call | solution.py:132
  142.9 73.3 %shard_map.50 = bf16[128,12288]{1,0:T(8,128)(2,1)} custom-call(s32[3]{0:T(128)} %pad_add_fusion.meta, bf16[128,12288]{1,0:T(8,128)(2,1)} %shard_map.49.kept_ref, bf16[128,3072]{1,0:T(8,128)(2,1)} %collective-permute-done.8.refs_0_, bf16[128,3072]{1,0:T(8,128)(2,1)} %collective-permute-done.7.refs_9_.refs_1_, ...), custom_call_target="tpu_custom_call", output_to_operand_aliasing={{}: (1, {})} | custom-call | tf_op jit(solution)/shard_map/pallas_call | solution.py:162
  (30 shorter events, 0.4 us)
Async XLA Ops:
  0.0 3.4 %copy-start.10 = (bf16[256,512]{1,0:T(8,128)(2,1)S(1)}, bf16[256,512]{1,0:T(8,128)(2,1)}, u32[]{:S(2)}) copy-start(bf16[256,512]{1,0:T(8,128)(2,1)} %param.5) | copy-start | bytes 786436
  0.0 3.4 %copy-start.9 = (bf16[256,512]{1,0:T(8,128)(2,1)S(1)}, bf16[256,512]{1,0:T(8,128)(2,1)}, u32[]{:S(2)}) copy-start(bf16[256,512]{1,0:T(8,128)(2,1)} %param.6) | copy-start | bytes 786436
  0.0 38.0 %copy-start.12 = (s32[4]{0:T(128)S(1)}, s32[4]{0:T(128)}, u32[]{:S(2)}) copy-start(s32[4]{0:T(128)} %param.7) | copy-start | bytes 52
  2.7 49.3 %collective-permute-start.5 = (bf16[256,3072]{1,0:T(8,128)(2,1)}, bf16[256,3072]{1,0:T(8,128)(2,1)}, u32[]{:S(2)}, u32[]{:S(2)}) collective-permute-start(bf16[256,3072]{1,0:T(8,128)(2,1)} %constant_dynamic-slice_fusion), channel_id=1, source_target_pairs={{0,2},{2,0},{4,6},{6,4},{8,10},{10,8},{12,14},{14,12},{16,18},{18,... | collective-permute-start | bytes 4718600 | tf_op jit(solution)/shard_map/ppermute | solution.py:227
  3.5 3.2 %collective-permute-start = (bf16[256,512]{1,0:T(8,128)(2,1)S(1)}, bf16[256,512]{1,0:T(8,128)(2,1)S(1)}, u32[]{:S(2)}, u32[]{:S(2)}) collective-permute-start(bf16[256,512]{1,0:T(8,128)(2,1)S(1)} %pad_maximum_fusion), channel_id=1, source_target_pairs={{0,2},{2,0},{4,6},{6,4},{8,10},{10,8},{12,14},{14,12},{16,18},{18,... | collective-permute-start | bytes 786440 | tf_op jit(solution)/shard_map/ppermute | solution.py:227
  6.7 0.7 copy-start.11
  7.4 63.0 %copy-start = (bf16[256,6144]{1,0:T(8,128)(2,1)S(1)}, bf16[256,6144]{1,0:T(8,128)(2,1)}, u32[]{:S(2)}) copy-start(bf16[256,6144]{1,0:T(8,128)(2,1)} %refs_1_.3) | copy-start | bytes 9437188
  8.7 15.4 %collective-permute-start.3 = (bf16[512,512]{1,0:T(8,128)(2,1)S(1)}, bf16[512,512]{1,0:T(8,128)(2,1)}, u32[]{:S(2)}, u32[]{:S(2)}) collective-permute-start(bf16[512,512]{1,0:T(8,128)(2,1)S(1)} %maximum_select_fusion.refs_6_), channel_id=1, source_target_pairs={{0,4},{2,6},{4,8},{6,10},{8,12},{10,14},{12,16},{14,18},{16,20},{1... | collective-permute-start | bytes 1572872 | tf_op jit(solution)/shard_map/ppermute | solution.py:230
  10.0 25.2 %collective-permute-start.1 = (bf16[512,512]{1,0:T(8,128)(2,1)S(1)}, bf16[512,512]{1,0:T(8,128)(2,1)S(1)}, u32[]{:S(2)}, u32[]{:S(2)}) collective-permute-start(bf16[512,512]{1,0:T(8,128)(2,1)S(1)} %maximum_select_fusion.refs_6_), channel_id=1, source_target_pairs={{0,8},{2,10},{4,12},{6,14},{8,16},{10,18},{12,20},{14,22},{16,24},... | collective-permute-start | bytes 1572872 | tf_op jit(solution)/shard_map/ppermute | solution.py:230
  11.3 0.8 copy-start.1
  24.1 28.0 %collective-permute-start.4 = (bf16[512,512]{1,0:T(8,128)(2,1)}, bf16[512,512]{1,0:T(8,128)(2,1)}, u32[]{:S(2)}, u32[]{:S(2)}) collective-permute-start(bf16[512,512]{1,0:T(8,128)(2,1)} %collective-permute-done.3.refs_5_), channel_id=1, source_target_pairs={{0,8},{2,10},{4,12},{6,14},{8,16},{10,18},{12,20},{14,22},{16,24},... | collective-permute-start | bytes 1572872 | tf_op jit(solution)/shard_map/ppermute | solution.py:230
  35.9 0.8 copy-start.5
  36.7 15.3 %collective-permute-start.2 = (bf16[256,512]{1,0:T(8,128)(2,1)}, bf16[256,512]{1,0:T(8,128)(2,1)S(1)}, u32[]{:S(2)}, u32[]{:S(2)}) collective-permute-start(bf16[256,512]{1,0:T(8,128)(2,1)} %slice.4), channel_id=1, source_target_pairs={{0,8},{2,10},{4,12},{6,14},{8,16},{10,18},{12,20},{14,22},{16,24},... | collective-permute-start | bytes 786440 | tf_op jit(solution)/shard_map/ppermute | solution.py:230
  52.0 1.0 copy-start.2
  53.1 1.0 copy-start.6
  54.1 16.3 %copy-start.7 = (bf16[512,512]{1,0:T(8,128)(2,1)S(1)}, bf16[512,512]{1,0:T(8,128)(2,1)}, u32[]{:S(2)}) copy-start(bf16[512,512]{1,0:T(8,128)(2,1)} %copy-done.5) | copy-start | bytes 1572868
  70.4 19.7 %copy-start.3 = (bf16[512,512]{1,0:T(8,128)(2,1)S(1)}, bf16[512,512]{1,0:T(8,128)(2,1)}, u32[]{:S(2)}) copy-start(bf16[512,512]{1,0:T(8,128)(2,1)} %copy-done.1) | copy-start | bytes 1572868
  87.4 20.7 %collective-permute-start.7 = (bf16[128,3072]{1,0:T(8,128)(2,1)}, bf16[128,3072]{1,0:T(8,128)(2,1)}, u32[]{:S(2)}, u32[]{:S(2)}) collective-permute-start(bf16[128,3072]{1,0:T(8,128)(2,1)} %shard_map.47.refs_7_), channel_id=1, source_target_pairs={{0,1},{1,0},{2,3},{3,2},{4,5},{5,4},{6,7},{7,6},{8,9},{9,8},{10,11... | collective-permute-start | bytes 2359304 | tf_op jit(solution)/shard_map/ppermute | solution.py:280
  87.7 36.2 %collective-permute-start.6 = (bf16[128,3072]{1,0:T(8,128)(2,1)}, bf16[128,3072]{1,0:T(8,128)(2,1)}, u32[]{:S(2)}, u32[]{:S(2)}) collective-permute-start(bf16[128,3072]{1,0:T(8,128)(2,1)} %shard_map.46.refs_7_), channel_id=1, source_target_pairs={{0,3},{1,2},{2,1},{3,0},{4,7},{5,6},{6,5},{7,4},{8,11},{9,10},{10,... | collective-permute-start | bytes 2359304 | tf_op jit(solution)/shard_map/ppermute | solution.py:280
  106.3 36.5 %collective-permute-start.8 = (bf16[128,3072]{1,0:T(8,128)(2,1)}, bf16[128,3072]{1,0:T(8,128)(2,1)}, u32[]{:S(2)}, u32[]{:S(2)}) collective-permute-start(bf16[128,3072]{1,0:T(8,128)(2,1)} %shard_map.48.refs_7_), channel_id=1, source_target_pairs={{0,2},{1,3},{2,0},{3,1},{4,6},{5,7},{6,4},{7,5},{8,10},{9,11},{10,... | collective-permute-start | bytes 2359304 | tf_op jit(solution)/shard_map/ppermute | solution.py:280
  123.9 1.0 copy-start.4
  124.9 1.0 copy-start.8
